TPU v7x, 32 devices: a whole 2x2x4 slice. The times are simulated.
32 devices in a mesh: lst: 4 (over y, x), night: 8 (over z, core).
Axes of the slice: x: 2, y: 2, z: 4, core: 2. Of those that a mesh axis runs over, the one named last changes fastest.
Arguments:
- visibility: bfloat16 [8, 32, 16, 2, 1536], P('night', 'lst'), may hold values from -18 to 18
- flags: int32 [8, 32, 16, 1536], P('night', 'lst'), may hold values 0 or 1
- counts: int32 [8, 32], P('night', 'lst'), may hold values from 1 to 4
- offsets: int32 [8], P('night'), may hold values from -6 to 6, as said below
- fraction: float32 [8], P('night'), may hold values from 0 to 1
- gains: float32 [8, 2, 1536], P('night'), may hold values from -6 to 6
- inverse_var: float32 [8, 1536], P('night'), may hold values from 0.005 to 0.05
- prior: float32 [1536], replicated, may hold values from 0.5 to 5
Outputs:
- binned: bfloat16 [32, 16, 2, 1536], P('lst')
- weight_total: float32 [32, 16, 1536], P('lst')
Inputs may be any that keep to these rules, and one draw needn't show every extreme that they name: `offsets`: both -6 and 6 occur among the nights.
All inputs are finite; a program needn't handle non-finite values. No bound on the sum of `flags` on one device may be relied on, other than what follows from the above.
Results may differ from a plain program's by a relative error of at most 0.009.
Values may be sent and summed in bfloat16 or wider, within the bound.
A program may use at most 64 MiB of HBM per device.

v0:
```python
import jax
import jax.numpy as jnp
from jax import lax
from jax.sharding import PartitionSpec as P


def extended(x, sides, width):
    for axis, dim in sides:
        size, length = (lax.axis_size(axis), x.shape[dim])
        up = [(i, (i + 1) % size) for i in range(size)]
        down = [(j, i) for i, j in up]
        last = lax.slice_in_dim(x, length - width, length, axis=dim)
        first = lax.slice_in_dim(x, 0, width, axis=dim)
        before = lax.ppermute(last, axis, up)
        after = lax.ppermute(first, axis, down)
        x = jnp.concatenate([before, x, after], axis=dim)
    return x


def spline_taps(fraction):
    cube = fraction * fraction * fraction
    square = fraction * fraction
    first = (1.0 - fraction) ** 3 / 6.0
    second = (3.0 * cube - 6.0 * square + 4.0) / 6.0
    third = (-3.0 * cube + 3.0 * square + 3.0 * fraction + 1.0) / 6.0
    fourth = cube / 6.0
    return jnp.stack([first, second, third, fourth], axis=-1)


def shards(visibility, flags, counts, offsets, fraction, gains, inverse_var, prior):
    local_nights = visibility.shape[0]
    sample_count = visibility.shape[1]
    baseline_count = visibility.shape[2]
    channel_count = visibility.shape[4]
    scale = (flags * counts[:, :, None, None]).astype(jnp.float32) * inverse_var[:, None, None, :]
    weight = scale.astype(jnp.bfloat16)
    real_part = visibility[:, :, :, 0].astype(jnp.float32)
    imag_part = visibility[:, :, :, 1].astype(jnp.float32)
    gain_re = gains[:, 0][:, None, None, :]
    gain_im = gains[:, 1][:, None, None, :]
    cal_re = gain_re * real_part - gain_im * imag_part
    cal_im = gain_re * imag_part + gain_im * real_part
    weighted = (scale[:, :, :, None, :] * jnp.stack([cal_re, cal_im], axis=3)).astype(jnp.bfloat16)
    stacked = jnp.concatenate([weighted, weight[:, :, :, None, :]], axis=3)
    taps = spline_taps(fraction)
    tap_index = jnp.arange(4).reshape(1, 1, 1, 4)
    shifts = offsets.reshape(1, local_nights, 1, 1)
    tap_values = taps.reshape(1, local_nights, 1, 4)
    padded_slab = extended(stacked, (("lst", 1),), sample_count)
    out_row = jnp.arange(sample_count).reshape(sample_count, 1, 1, 1)
    source = jnp.arange(3 * sample_count).reshape(1, 1, 3 * sample_count, 1)
    target = out_row - shifts + tap_index - 1 + sample_count
    matrix = jnp.sum(jnp.where(source == target, tap_values, 0.0), axis=-1).astype(jnp.bfloat16)
    partial_numerator = jnp.dot(
        matrix.reshape(sample_count, local_nights * 3 * sample_count),
        padded_slab.reshape(local_nights * 3 * sample_count, baseline_count * 3 * channel_count),
        preferred_element_type=jnp.float32,
    )
    partial_numerator = partial_numerator.reshape(sample_count, baseline_count, 3, channel_count)
    totals = lax.psum(partial_numerator, "night")
    denominator_sum = totals[:, :, 2]
    binned = (
        totals[:, :, 0:2] / (denominator_sum[:, :, None, :] + prior[None, None, None, :])
    ).astype(jnp.bfloat16)
    return (binned, denominator_sum)


def solution(mesh):
    in_specs = (
        P("night", "lst", None, None, None),
        P("night", "lst", None, None),
        P("night", "lst"),
        P("night"),
        P("night"),
        P("night", None, None),
        P("night", None),
        P(),
    )
    out_specs = (P("lst", None, None, None), P("lst", None, None))
    return jax.shard_map(shards, mesh=mesh, in_specs=in_specs, out_specs=out_specs, check_vma=False)
```

profile of v0, /device:TPU:0, one launch (start us, length us, event | category | flops | bytes accessed | tf_op | source)
XLA Modules:
  0.0 172.8 jit_solution(5491326670959882846)
XLA Ops:
  7.2 0.0 copy-start.3
  7.2 0.0 copy-start.1
  7.2 0.0 copy-start.4
  7.2 0.0 all-reduce.2.cloned.1.call-start
  7.2 0.8 slice_reduce_fusion.1
  8.1 3.0 %fusion.11 = (bf16[1,8,16,1,1536]{4,3,2,1,0:T(2,128)(2,1)S(1)}, bf16[1,8,16,1,1536]{4,3,2,1,0:T(2,128)(2,1)S(1)}) fusion(bf16[1,8,16,2,1536]{4,3,2,1,0:T(2,128)(2,1)} %param.8), kind=kLoop, calls=%fused_computation.29 | loop fusion | bytes 1572864 | tf_op jit(solution)/shard_map/slice | solution.py:37
  11.1 0.0 copy-done.3
  11.2 0.0 copy-done.1
  11.2 0.0 copy-done.4
  11.2 0.2 fusion.7
  11.4 0.3 fusion.4
  11.7 0.1 fusion.3
  11.8 0.1 pad_maximum_fusion.1
  11.9 3.9 %collective-permute-start.1 = (bf16[1,8,16,3,1536]{4,2,3,1,0:T(8,128)(2,1)S(1)}, bf16[1,8,16,3,1536]{4,2,3,1,0:T(8,128)(2,1)S(1)}, u32[]{:S(2)}, u32[]{:S(2)}) collective-permute-start(bf16[1,8,16,3,1536]{4,2,3,1,0:T(8,128)(2,1)S(1)} %pad_maximum_fusion.1), channel_id=1, source_target_pairs={{8,0},{16,8},{24,16},{0,24},{9,1},{17,9},{25,17},{1,25},{10,2},{18... | collective-permute-start | bytes 3538952 | tf_op jit(solution)/shard_map/ppermute | solution.py:15
  15.9 0.0 collective-permute-start
  17.2 0.1 maximum_bitcast_fusion
  17.3 0.1 select_reduce_fusion
  17.4 24.9 %collective-permute-done.1 = bf16[1,8,16,3,1536]{4,2,3,1,0:T(8,128)(2,1)S(1)} collective-permute-done((bf16[1,8,16,3,1536]{4,2,3,1,0:T(8,128)(2,1)S(1)}, bf16[1,8,16,3,1536]{4,2,3,1,0:T(8,128)(2,1)S(1)}, u32[]{:S(2)}, u32[]{:S(2)}) %collective-permute-start.1) | collective-permute-done | bytes 1179680 | tf_op jit(solution)/shard_map/ppermute | solution.py:15
  42.3 25.1 %collective-permute-done = bf16[1,8,16,3,1536]{4,2,3,1,0:T(8,128)(2,1)S(1)} collective-permute-done((bf16[1,8,16,3,1536]{4,2,3,1,0:T(8,128)(2,1)S(1)}, bf16[1,8,16,3,1536]{4,2,3,1,0:T(8,128)(2,1)S(1)}, u32[]{:S(2)}, u32[]{:S(2)}) %collective-permute-start) | collective-permute-done | bytes 1179680 | tf_op jit(solution)/shard_map/ppermute | solution.py:14
  67.4 0.4 pad_maximum_fusion
  67.8 5.4 %copy.25 = bf16[1,24,16,3,1536]{4,3,2,1,0:T(4,128)(2,1)} copy(bf16[1,24,16,3,1536]{4,2,3,1,0:T(8,128)(2,1)S(1)} %pad_maximum_fusion) | data formatting | bytes 7077888 | tf_op jit(solution)/shard_map/concatenate | solution.py:16
  73.2 6.2 %reshape.136 = bf16[24,73728]{1,0:T(8,128)(2,1)S(1)} reshape(bf16[1,24,16,3,1536]{4,3,2,1,0:T(4,128)(2,1)} %copy.25) | data formatting | bytes 7077888 | tf_op jit(solution)/shard_map/reshape | solution.py:56
  79.4 6.2 %dot_general.8 = bf16[16,3,1536,24]{2,1,0,3:T(4,128)(2,1)} reshape(bf16[73728,24]{0,1:T(8,128)(2,1)S(1)} %bitcast.25) | data formatting | bytes 7077888 | tf_op jit(solution)/shard_map/dot_general | solution.py:54
  85.6 8.3 %fusion = f32[8,16,3,1536]{3,0,2,1:T(8,128)} fusion(bf16[16,3,1536,24]{2,1,0,3:T(4,128)(2,1)} %dot_general.8, bf16[8,24]{1,0:T(8,128)(2,1)S(1)} %select_reduce_fusion), kind=kOutput, calls=%fused_computation.1 | convolution fusion | flops 28311552 | bytes 5898624 | tf_op jit(solution)/shard_map/dot_general | solution.py:54
  93.8 0.0 copy-start.2
  93.8 0.0 all-reduce.2.cloned.1.call-update
  93.9 67.2 %all-reduce.2.cloned.1.call-done = f32[8,16,3,1536]{3,0,2,1:T(8,128)} async-done(((f32[8,16,3,1536]{3,0,2,1:T(8,128)}), f32[8,16,3,1536]{3,0,2,1:T(8,128)}) %all-reduce.2.cloned.1.call-update) | async-done | bytes 2359312 | tf_op jit(solution)/shard_map/psum | solution.py:60
  161.0 0.0 copy-done.2
  161.0 0.0 copy-start
  161.0 1.4 slice_bitcast_fusion
  162.5 0.4 copy-done
  162.9 0.2 fusion.2
  163.1 1.5 copy.27
  164.6 1.3 copy.28
  (3 shorter events, 0.0 us)
Async XLA Ops:
  7.2 4.0 %copy-start.3 = (f32[1,1536]{1,0:T(1,128)S(1)}, f32[1,1536]{1,0:T(1,128)}, u32[]{:S(2)}) copy-start(f32[1,1536]{1,0:T(1,128)} %param.14) | copy-start | bytes 18436
  7.2 4.0 %copy-start.1 = (s32[1,8,16,1536]{3,2,1,0:T(8,128)S(1)}, s32[1,8,16,1536]{3,2,1,0:T(8,128)}, u32[]{:S(2)}) copy-start(s32[1,8,16,1536]{3,2,1,0:T(8,128)} %param.9) | copy-start | bytes 2359300
  7.2 4.0 %copy-start.4 = (s32[1,8]{1,0:T(1,128)S(1)}, s32[1,8]{1,0:T(1,128)}, u32[]{:S(2)}) copy-start(s32[1,8]{1,0:T(1,128)} %param.10) | copy-start | bytes 100
  7.2 153.8 %all-reduce.2.cloned.1.call-start = ((), (), s32[]{:S(2)}) async-start(), calls=%async_computation | async-start | bytes 4718592 | tf_op jit(solution)/shard_map/psum | solution.py:60
  11.9 30.3 %collective-permute-start.1 = (bf16[1,8,16,3,1536]{4,2,3,1,0:T(8,128)(2,1)S(1)}, bf16[1,8,16,3,1536]{4,2,3,1,0:T(8,128)(2,1)S(1)}, u32[]{:S(2)}, u32[]{:S(2)}) collective-permute-start(bf16[1,8,16,3,1536]{4,2,3,1,0:T(8,128)(2,1)S(1)} %pad_maximum_fusion.1), channel_id=1, source_target_pairs={{8,0},{16,8},{24,16},{0,24},{9,1},{17,9},{25,17},{1,25},{10,2},{18... | collective-permute-start | bytes 3538952 | tf_op jit(solution)/shard_map/ppermute | solution.py:15
  15.9 51.5 %collective-permute-start = (bf16[1,8,16,3,1536]{4,2,3,1,0:T(8,128)(2,1)S(1)}, bf16[1,8,16,3,1536]{4,2,3,1,0:T(8,128)(2,1)S(1)}, u32[]{:S(2)}, u32[]{:S(2)}) collective-permute-start(bf16[1,8,16,3,1536]{4,2,3,1,0:T(8,128)(2,1)S(1)} %pad_maximum_fusion.1), channel_id=1, source_target_pairs={{0,8},{8,16},{16,24},{24,0},{1,9},{9,17},{17,25},{25,1},{2,10},{10... | collective-permute-start | bytes 3538952 | tf_op jit(solution)/shard_map/ppermute | solution.py:14
  93.8 67.2 %copy-start.2 = (f32[1536]{0:T(1024)S(1)}, f32[1536]{0:T(1024)}, u32[]{:S(2)}) copy-start(f32[1536]{0:T(1024)} %param.15) | copy-start | bytes 18436
  161.0 1.9 %copy-start = (f32[8,16,3,1536]{3,0,2,1:T(8,128)S(1)}, f32[8,16,3,1536]{3,0,2,1:T(8,128)}, u32[]{:S(2)}) copy-start(f32[8,16,3,1536]{3,0,2,1:T(8,128)} %all-reduce.2.cloned.1.call-done) | copy-start | bytes 7077892
Sparse Core Ops, SparseCore 0:
  94.0 67.0 all-reduce.1
where the time goes:
time: 173 us
  waiting for transfers between devices  117 us (68%)
  local copies, waits for them, and re-layouts  24.9 us (14%)
  between operations  15.5 us (9%)
  matrix products  8.26 us (5%)
  starting transfers between devices  3.99 us (2%)
  other arithmetic  2.95 us (2%)
    psum x1, waiting for transfers between devices, shards(): totals = lax.psum(partial_numerator, 'night')  67.2 us
    ppermute x1, waiting for transfers between devices, extended(): before = lax.ppermute(last, axis, up)  25.1 us
    ppermute x1, waiting for transfers between devices, extended(): after = lax.ppermute(first, axis, down)  24.9 us
    dot_general x1, matrix products, shards(): jnp.dot(matrix.reshape(sample_count, local_nights * 3 * sample_count), pa...  8.26 us
    dot_general x1, local copies, waits for them, and re-layouts, shards(): jnp.dot(matrix.reshape(sample_count, local_nights * 3 * sample_count), pa...  6.2 us
    reshape x1, local copies, waits for them, and re-layouts, shards(): padded_slab.reshape(local_nights * 3 * sample_count, baseline_count * 3 *...  6.2 us
    concatenate x1, local copies, waits for them, and re-layouts, extended(): x = jnp.concatenate([before, x, after], axis=dim)  5.36 us
    ppermute x1, starting transfers between devices, extended(): after = lax.ppermute(first, axis, down)  3.95 us
  transfers between devices with their start and end apart: 3, of which 3 were waited for; matrix products, arithmetic and copies ran while one was open for 0% of the time, Pallas kernels for 0%

commit v1 on v0

v1 whole, which is shorter than its diff:
```python
import functools
import math

import jax
import jax.numpy as jnp
from jax import lax
from jax.experimental import pallas as pl
from jax.experimental.pallas import tpu as pltpu
from jax.sharding import PartitionSpec as P

LANES = 128
REACH = 7
SHIFTS = 16


def spline_taps(fraction):
    cube = fraction * fraction * fraction
    square = fraction * fraction
    first = (1.0 - fraction) ** 3 / 6.0
    second = (3.0 * cube - 6.0 * square + 4.0) / 6.0
    third = (-3.0 * cube + 3.0 * square + 3.0 * fraction + 1.0) / 6.0
    fourth = cube / 6.0
    return jnp.stack([first, second, third, fourth], axis=-1)


def kernel(
    lsts, chips, rows, blocks,
    coef_ref, slab_ref, prior_ref, out_ref,
    ext, pair_out, pair_in, own, sum_out, sum_in,
    near_s, near_r, far_s, far_r, pair_s, pair_r, sum_s, sum_r, gat_s, gat_r, fwd_s, fwd_r,
):
    lst = lax.axis_index("lst")
    night = lax.axis_index("night")
    chip = night // 2
    core = night % 2
    partner = night + 1 - 2 * core
    groups = math.gcd(blocks, chips)
    splits = chips // groups
    phases = blocks // groups
    part = rows // splits
    piece = part // 2
    two_hops = lsts == 4
    if two_hops:
        odd = lst % 2
        near_to, near_at = lst + 1 - 2 * odd, 2 * odd * rows
        far_to, far_at = (lst + 2) % 4, 2 * odd * rows
        far_from = (2 - 2 * odd) * rows
    else:
        near_to, near_at = (lst + 1) % lsts, 0
        far_to, far_at = (lst + lsts - 1) % lsts, 2 * rows
        far_from = rows

    def remote(src, dst, send, recv, l, n):
        return pltpu.make_async_remote_copy(
            src_ref=src, dst_ref=dst, send_sem=send, recv_sem=recv,
            device_id={"lst": l, "night": n}, device_id_type=pl.DeviceIdType.MESH)

    others = [((chip + d) % chips) * 2 + core for d in range(1, chips)]
    barrier = pltpu.get_barrier_semaphore()
    greeted = [(near_to, night), (far_to, night), (lst, partner)] + [(lst, n) for n in others]
    for l, n in greeted:
        pl.semaphore_signal(barrier, inc=1, device_id={"lst": l, "night": n}, device_id_type=pl.DeviceIdType.MESH)
    pl.semaphore_wait(barrier, len(greeted))

    def lanes(block):
        return pl.ds(pl.multiple_of(block * LANES, LANES), LANES)

    def near(t):
        return remote(ext.at[t, pl.ds(rows, rows)], ext.at[t, pl.ds(near_at, rows)],
                      near_s.at[t], near_r.at[t], near_to, night)

    def far(t):
        return remote(ext.at[t, pl.ds(far_from, rows)], ext.at[t, pl.ds(far_at, rows)],
                      far_s.at[t], far_r.at[t], far_to, night)

    def pass_on(t):
        near(t).wait_recv()
        if two_hops:
            far(t).start()

    def pair(s):
        return remote(pair_out.at[s], pair_in.at[s], pair_s.at[s], pair_r.at[s], lst, partner)

    def target(s):
        g, r = (s % chips) // splits, s % splits
        return (chip + 1 + g) % groups + ((chip // groups + 1 + r) % splits) * groups

    def toward(s):
        return remote(sum_out.at[s], sum_in.at[s], sum_s.at[s], sum_r.at[s], lst, target(s) * 2 + core)

    def place(owner, p, of_core):
        block = (owner % groups) * phases + p
        row = (owner // groups) * part + of_core * piece
        return out_ref.at[pl.ds(row, piece), :, :, lanes(block)]

    def gather(p, d):
        here = place(chip, p, core)
        i = p * chips + d
        return remote(here, here, gat_s.at[i], gat_r.at[i], lst, others[d - 1])

    def forward(p, d):
        here = place((chip + chips - d) % chips, p, core)
        i = p * chips + d
        return remote(here, here, fwd_s.at[i], fwd_r.at[i], lst, partner)

    def regrid(s, base, dst, index):
        t = s // splits

        def component(c, carry):
            acc = jnp.zeros((piece,) + ext.shape[3:], jnp.float32)
            for d in range(SHIFTS):
                window = ext[t, pl.ds(rows - REACH + d + base, piece), c]
                acc = acc + coef_ref[0, d] * window.astype(jnp.float32)
            dst[index, :, c] = acc.astype(dst.dtype)
            return carry

        lax.fori_loop(0, 3, component, 0)

    def first_part(s):
        base = ((chip // groups + 1 + s % splits) % splits) * part
        regrid(s, base + (1 - core) * piece, pair_out, s)
        pair(s).start()
        regrid(s, base + core * piece, own, s)

    def pair_sum(s):
        pair(s).wait_recv()
        both = own[s] + pair_in[s].astype(jnp.float32)
        if s % chips < chips - 1:
            sum_out[s] = both.astype(jnp.bfloat16)
            toward(s).start()
        else:
            own[s] = both

    def finish(p):
        total = own[p * chips + chips - 1]
        for k in range(chips - 1):
            toward(p * chips + k).wait_recv()
            total = total + sum_in[p * chips + k].astype(jnp.float32)
        block = (chip % groups) * phases + p
        prior = prior_ref[:, lanes(block)]
        den = total[:, 2]
        inverse = (den + prior[None])[:, None]
        row = (chip // groups) * part + core * piece
        out_ref[pl.ds(row, piece), 0:2, :, lanes(block)] = (total[:, 0:2] / inverse).astype(jnp.bfloat16)
        out_ref[pl.ds(row, piece), 2:3, :, lanes(block)] = den[:, None].astype(jnp.bfloat16)
        for d in range(1, chips):
            gather(p, d).start()
        forward(p, 0).start()

    def share(p):
        for d in range(1, chips):
            gather(p, d).wait_recv()
            forward(p, d).start()

    for t in range(blocks):
        block = ((chip + 1 + t % groups) % groups) * phases + t // groups
        ext[t, rows:2 * rows] = slab_ref[:, :, :, lanes(block)]
        near(t).start()
        if not two_hops:
            far(t).start()

    steps = phases * chips
    pass_on(0)
    for s in range(steps):
        t, p, k = s // splits, s // chips, s % chips
        if s % splits == 0:
            if t + 1 < blocks:
                pass_on(t + 1)
            far(t).wait_recv()
        first_part(s)
        if s > 0:
            pair_sum(s - 1)
        if p > 0 and k == min(1, chips - 1):
            finish(p - 1)
        if p > 0 and k == chips - 1:
            share(p - 1)
    pair_sum(steps - 1)
    finish(phases - 1)
    share(phases - 1)
    for p in range(phases):
        for d in range(chips):
            forward(p, d).wait()
            if d > 0:
                gather(p, d).wait_send()
    for s in range(steps):
        pair(s).wait_send()
        if s % chips < chips - 1:
            toward(s).wait_send()
    for t in range(blocks):
        near(t).wait_send()
        far(t).wait_send()


def shards(mesh, visibility, flags, counts, offsets, fraction, gains, inverse_var, prior):
    lsts, chips = mesh.shape["lst"], mesh.shape["night"] // 2
    rows, baselines, channels = visibility.shape[1], visibility.shape[2], visibility.shape[4]
    blocks = channels // LANES
    scale = (flags[0] * counts[0][:, None, None]).astype(jnp.float32) * inverse_var[0][None, None, :]
    weight = scale.astype(jnp.bfloat16)
    real_part = visibility[0, :, :, 0].astype(jnp.float32)
    imag_part = visibility[0, :, :, 1].astype(jnp.float32)
    gain_re, gain_im = gains[0, 0], gains[0, 1]
    cal_re = gain_re * real_part - gain_im * imag_part
    cal_im = gain_re * imag_part + gain_im * real_part
    slab = jnp.stack([(scale * cal_re).astype(jnp.bfloat16), (scale * cal_im).astype(jnp.bfloat16), weight], axis=1)
    taps = spline_taps(fraction)[0].astype(jnp.bfloat16).astype(jnp.float32)
    shift = jnp.arange(SHIFTS).reshape(SHIFTS, 1)
    wanted = jnp.arange(4).reshape(1, 4) - offsets[0] - 1 + REACH
    coef = jnp.sum(jnp.where(shift == wanted, taps[None, :], 0.0), axis=1).reshape(1, SHIFTS)

    groups = math.gcd(blocks, chips)
    splits = chips // groups
    phases = blocks // groups
    steps = phases * chips
    piece = rows // splits // 2
    tile = (piece, 3, baselines, LANES)
    dma = pltpu.SemaphoreType.DMA
    out = pl.pallas_call(
        functools.partial(kernel, lsts, chips, rows, blocks),
        out_shape=jax.ShapeDtypeStruct((rows, 3, baselines, channels), jnp.bfloat16),
        in_specs=[
            pl.BlockSpec(memory_space=pltpu.SMEM),
            pl.BlockSpec(memory_space=pltpu.VMEM),
            pl.BlockSpec(memory_space=pltpu.VMEM),
        ],
        out_specs=pl.BlockSpec(memory_space=pltpu.VMEM),
        scratch_shapes=[
            pltpu.VMEM((blocks, 3 * rows, 3, baselines, LANES), jnp.bfloat16),
            pltpu.VMEM((steps,) + tile, jnp.bfloat16),
            pltpu.VMEM((steps,) + tile, jnp.bfloat16),
            pltpu.VMEM((steps,) + tile, jnp.float32),
            pltpu.VMEM((steps,) + tile, jnp.bfloat16),
            pltpu.VMEM((steps,) + tile, jnp.bfloat16),
            dma((blocks,)), dma((blocks,)), dma((blocks,)), dma((blocks,)),
            dma((steps,)), dma((steps,)), dma((steps,)), dma((steps,)),
            dma((steps,)), dma((steps,)), dma((steps,)), dma((steps,)),
        ],
        compiler_params=pltpu.CompilerParams(
            collective_id=0, has_side_effects=True, vmem_limit_bytes=40 * 2**20),
    )(coef, slab, prior.reshape(1, channels))
    binned = jnp.swapaxes(out[:, 0:2], 1, 2)
    return binned, out[:, 2].astype(jnp.float32)


def solution(mesh):
    in_specs = (
        P("night", "lst", None, None, None),
        P("night", "lst", None, None),
        P("night", "lst"),
        P("night"),
        P("night"),
        P("night", None, None),
        P("night", None),
        P(),
    )
    out_specs = (P("lst", None, None, None), P("lst", None, None))
    return jax.shard_map(functools.partial(shards, mesh), mesh=mesh, in_specs=in_specs, out_specs=out_specs, check_vma=False)
```

time: 173 us -> 63.7 us (0.37)
  waiting for transfers between devices: 117 us -> 0 us
  Pallas kernels: 0 us -> 54.3 us
  local copies, waits for them, and re-layouts: 24.9 us -> 5.42 us
  between operations: 15.5 us -> 2.09 us
  matrix products: 8.26 us -> 0 us
  starting transfers between devices: 3.99 us -> 0 us
    psum x1 -> x0, waiting for transfers between devices: 67.2 us -> none  [shards(): totals = lax.psum(partial_numerator, 'night')]
    pallas_call x0 -> x1, Pallas kernels: none -> 54.3 us  [shards(): pl.pallas_call(functools.partial(kernel, lsts, chips, rows, blocks), out_...]
    ppermute x2 -> x0, waiting for transfers between devices: 50 us -> none  [the longest x1 25.1 us: extended(): before = lax.ppermute(last, axis, up)]
    dot_general x1 -> x0, matrix products: 8.26 us -> none  [shards(): jnp.dot(matrix.reshape(sample_count, local_nights * 3 * sample_count), pa...]
    dot_general x1 -> x0, local copies, waits for them, and re-layouts: 6.2 us -> none  [shards(): jnp.dot(matrix.reshape(sample_count, local_nights * 3 * sample_count), pa...]
    reshape x1, local copies, waits for them, and re-layouts: 6.2 us -> 0.01 us  [shards(): prior.reshape(1, channels)]
    concatenate x1 -> x0, local copies, waits for them, and re-layouts: 5.36 us -> none  [extended(): x = jnp.concatenate([before, x, after], axis=dim)]
    ppermute x2 -> x0, starting transfers between devices: 3.95 us -> none  [the longest x1 3.95 us: extended(): after = lax.ppermute(first, axis, down)]
  transfers between devices with their start and end apart: 3 -> 0, of which waited for: 3 -> 0; matrix products, arithmetic and copies ran while one was open for 0% -> 0% of each run, Pallas kernels for 0% -> 0%
where the time goes in v1:
time: 63.7 us; the launch traced here: 63.5 us
  Pallas kernels  54.3 us (85%)
  local copies, waits for them, and re-layouts  5.42 us (9%)
  between operations  2.09 us (3%)
  other arithmetic  1.69 us (3%)
    pallas_call x1, Pallas kernels, shards(): pl.pallas_call(functools.partial(kernel, lsts, chips, rows, blocks), out_...  54.3 us
    slice x1, local copies, waits for them, and re-layouts, shards(): imag_part = visibility[0, :, :, 1].astype(jnp.float32)  3.06 us
    unnamed x11, local copies, waits for them, and re-layouts  2.27 us

profile of v1, /device:TPU:0, one launch (start us, length us, event | category | flops | bytes accessed | tf_op | source)
XLA Modules:
  0.0 63.5 jit_solution(18438556721255220915)
XLA Ops:
  1.3 0.1 maximum_convert_fusion
  2.1 0.1 select_reduce_fusion
  2.1 0.0 copy-start.1
  2.1 0.0 copy-start.3
  2.1 0.0 copy-start
  2.2 0.0 copy-start.4
  2.2 3.1 %fusion.9 = (bf16[1,8,16,1,1536]{4,3,2,1,0:T(2,128)(2,1)S(1)}, bf16[1,8,16,1,1536]{4,3,2,1,0:T(2,128)(2,1)S(1)}) fusion(bf16[1,8,16,2,1536]{4,3,2,1,0:T(2,128)(2,1)} %param.8), kind=kLoop, calls=%fused_computation.25 | loop fusion | bytes 1572864 | tf_op jit(solution)/shard_map/slice | solution.py:201
  5.2 0.0 copy-done.1
  5.3 0.0 copy-done.3
  5.3 0.0 copy-done
  5.3 0.0 copy-done.4
  5.3 0.4 fusion.2
  5.8 0.0 copy-start.2
  5.8 0.1 pad_maximum_fusion.slab_ref
  5.9 0.6 copy-done.2
  6.5 54.3 %shard_map.95 = bf16[8,3,16,1536]{3,2,1,0:T(8,128)(2,1)S(1)} custom-call(f32[1,16]{1,0:T(1,128)S(1)} %bitcast.35, bf16[8,3,16,1536]{3,2,1,0:T(8,128)(2,1)S(1)} %pad_maximum_fusion.slab_ref, f32[1,1536]{1,0:T(1,128)S(1)} %reshape.140.prior_ref), custom_call_target="tpu_custom_call" | custom-call | tf_op jit(solution)/shard_map/pallas_call | solution.py:218
  60.8 0.1 slice_bitcast_fusion
  60.9 1.7 %copy.15 = bf16[8,16,2,1536]{3,2,1,0:T(2,128)(2,1)} copy(bf16[8,16,2,1536]{3,1,2,0:T(8,128)(2,1)S(1)} %slice_bitcast_fusion) | data formatting | bytes 1572864
  62.6 1.0 %bitcast_convert_fusion = f32[8,16,1536]{2,1,0:T(8,128)} fusion(bf16[8,3,16,1536]{3,2,1,0:T(8,128)(2,1)S(1)} %shard_map.95), kind=kLoop, calls=%fused_computation.18 | loop fusion | flops 196608 | bytes 1179648 | tf_op jit(solution)/shard_map/convert_element_type | solution.py:242
  (4 shorter events, 0.1 us)
Async XLA Ops:
  2.1 3.1 %copy-start.1 = (f32[1,2,1536]{2,1,0:T(2,128)S(1)}, f32[1,2,1536]{2,1,0:T(2,128)}, u32[]{:S(2)}) copy-start(f32[1,2,1536]{2,1,0:T(2,128)} %param.13) | copy-start | bytes 36868
  2.1 3.1 %copy-start.3 = (f32[1,1536]{1,0:T(1,128)S(1)}, f32[1,1536]{1,0:T(1,128)}, u32[]{:S(2)}) copy-start(f32[1,1536]{1,0:T(1,128)} %param.14) | copy-start | bytes 18436
  2.1 3.2 %copy-start = (s32[1,8,16,1536]{3,2,1,0:T(8,128)S(1)}, s32[1,8,16,1536]{3,2,1,0:T(8,128)}, u32[]{:S(2)}) copy-start(s32[1,8,16,1536]{3,2,1,0:T(8,128)} %param.9) | copy-start | bytes 2359300
  2.2 3.2 %copy-start.4 = (s32[1,8]{1,0:T(1,128)S(1)}, s32[1,8]{1,0:T(1,128)}, u32[]{:S(2)}) copy-start(s32[1,8]{1,0:T(1,128)} %param.10) | copy-start | bytes 100
  5.8 0.7 %copy-start.2 = (f32[1536]{0:T(1024)S(1)}, f32[1536]{0:T(1024)}, u32[]{:S(2)}) copy-start(f32[1536]{0:T(1024)} %param.15) | copy-start | bytes 18436

commit v2 on v1

--- a/solution.py
+++ b/solution.py
@@ -25,7 +25,7 @@
 
 def kernel(
     lsts, chips, rows, blocks,
-    coef_ref, slab_ref, prior_ref, out_ref,
+    coef_ref, vis_ref, flags_ref, level_ref, gains_ref, prior_ref, out_ref,
     ext, pair_out, pair_in, own, sum_out, sum_in,
     near_s, near_r, far_s, far_r, pair_s, pair_r, sum_s, sum_r, gat_s, gat_r, fwd_s, fwd_r,
 ):
@@ -60,7 +60,6 @@
     greeted = [(near_to, night), (far_to, night), (lst, partner)] + [(lst, n) for n in others]
     for l, n in greeted:
         pl.semaphore_signal(barrier, inc=1, device_id={"lst": l, "night": n}, device_id_type=pl.DeviceIdType.MESH)
-    pl.semaphore_wait(barrier, len(greeted))
 
     def lanes(block):
         return pl.ds(pl.multiple_of(block * LANES, LANES), LANES)
@@ -154,26 +153,40 @@
 
     for t in range(blocks):
         block = ((chip + 1 + t % groups) % groups) * phases + t // groups
-        ext[t, rows:2 * rows] = slab_ref[:, :, :, lanes(block)]
+        scale = flags_ref[:, :, lanes(block)].astype(jnp.float32) * level_ref[:, :, lanes(block)]
+        real_part = vis_ref[:, 0, :, lanes(block)].astype(jnp.float32)
+        imag_part = vis_ref[:, 1, :, lanes(block)].astype(jnp.float32)
+        gain_re = gains_ref[0:1, lanes(block)][None]
+        gain_im = gains_ref[1:2, lanes(block)][None]
+        cal_re = gain_re * real_part - gain_im * imag_part
+        cal_im = gain_re * imag_part + gain_im * real_part
+        ext[t, rows:2 * rows, 0] = (scale * cal_re).astype(jnp.bfloat16)
+        ext[t, rows:2 * rows, 1] = (scale * cal_im).astype(jnp.bfloat16)
+        ext[t, rows:2 * rows, 2] = scale.astype(jnp.bfloat16)
+    pl.semaphore_wait(barrier, len(greeted))
+
+    for t in range(blocks):
         near(t).start()
         if not two_hops:
             far(t).start()
 
     steps = phases * chips
-    pass_on(0)
+    for t in range(min(1, blocks)):
+        pass_on(t)
     for s in range(steps):
         t, p, k = s // splits, s // chips, s % chips
         if s % splits == 0:
             if t + 1 < blocks:
                 pass_on(t + 1)
-            far(t).wait_recv()
-        first_part(s)
         if s > 0:
             pair_sum(s - 1)
         if p > 0 and k == min(1, chips - 1):
             finish(p - 1)
         if p > 0 and k == chips - 1:
             share(p - 1)
+        if s % splits == 0:
+            far(t).wait_recv()
+        first_part(s)
     pair_sum(steps - 1)
     finish(phases - 1)
     share(phases - 1)
@@ -195,14 +208,7 @@
     lsts, chips = mesh.shape["lst"], mesh.shape["night"] // 2
     rows, baselines, channels = visibility.shape[1], visibility.shape[2], visibility.shape[4]
     blocks = channels // LANES
-    scale = (flags[0] * counts[0][:, None, None]).astype(jnp.float32) * inverse_var[0][None, None, :]
-    weight = scale.astype(jnp.bfloat16)
-    real_part = visibility[0, :, :, 0].astype(jnp.float32)
-    imag_part = visibility[0, :, :, 1].astype(jnp.float32)
-    gain_re, gain_im = gains[0, 0], gains[0, 1]
-    cal_re = gain_re * real_part - gain_im * imag_part
-    cal_im = gain_re * imag_part + gain_im * real_part
-    slab = jnp.stack([(scale * cal_re).astype(jnp.bfloat16), (scale * cal_im).astype(jnp.bfloat16), weight], axis=1)
+    level = (counts[0].astype(jnp.float32)[:, None] * inverse_var[0][None, :])[:, None, :]
     taps = spline_taps(fraction)[0].astype(jnp.bfloat16).astype(jnp.float32)
     shift = jnp.arange(SHIFTS).reshape(SHIFTS, 1)
     wanted = jnp.arange(4).reshape(1, 4) - offsets[0] - 1 + REACH
@@ -220,9 +226,7 @@
         out_shape=jax.ShapeDtypeStruct((rows, 3, baselines, channels), jnp.bfloat16),
         in_specs=[
             pl.BlockSpec(memory_space=pltpu.SMEM),
-            pl.BlockSpec(memory_space=pltpu.VMEM),
-            pl.BlockSpec(memory_space=pltpu.VMEM),
-        ],
+        ] + [pl.BlockSpec(memory_space=pltpu.VMEM)] * 5,
         out_specs=pl.BlockSpec(memory_space=pltpu.VMEM),
         scratch_shapes=[
             pltpu.VMEM((blocks, 3 * rows, 3, baselines, LANES), jnp.bfloat16),
@@ -237,7 +241,7 @@
         ],
         compiler_params=pltpu.CompilerParams(
             collective_id=0, has_side_effects=True, vmem_limit_bytes=40 * 2**20),
-    )(coef, slab, prior.reshape(1, channels))
+    )(coef, jnp.swapaxes(visibility[0], 1, 2), flags[0], level, gains[0], prior.reshape(1, channels))
     binned = jnp.swapaxes(out[:, 0:2], 1, 2)
     return binned, out[:, 2].astype(jnp.float32)
 

time: 63.7 us -> 61.1 us (0.959)
  Pallas kernels: 54.3 us -> 52.4 us
  local copies, waits for them, and re-layouts: 5.42 us -> 3.7 us
  other arithmetic: 1.69 us -> 2.59 us
    slice x2 -> x0, local copies, waits for them, and re-layouts: 3.09 us -> none  [the longest x1 3.06 us: shards(): imag_part = visibility[0, :, :, 1].astype(jnp.float32)]
    pallas_call x1, Pallas kernels: 54.3 us -> 52.4 us  [shards(): pl.pallas_call(functools.partial(kernel, lsts, chips, rows, blocks), out_...]
    reshape x1, local copies, waits for them, and re-layouts: 0.01 us -> 0.7 us  [shards(): prior.reshape(1, channels)]
    unnamed x1, other arithmetic: 0.02 us -> 0.71 us
    unnamed x11 -> x6, local copies, waits for them, and re-layouts: 2.27 us -> 2.94 us
where the time goes in v2:
time: 61.1 us; the launch traced here: 60.8 us
  Pallas kernels  52.4 us (86%)
  local copies, waits for them, and re-layouts  3.7 us (6%)
  other arithmetic  2.59 us (4%)
  between operations  2.1 us (3%)
    pallas_call x1, Pallas kernels, shards(): pl.pallas_call(functools.partial(kernel, lsts, chips, rows, blocks), out_...  52.4 us
    unnamed x6, local copies, waits for them, and re-layouts  2.94 us

profile of v2, /device:TPU:0, one launch (start us, length us, event | category | flops | bytes accessed | tf_op | source)
XLA Modules:
  0.0 60.8 jit_solution(4537057270062704824)
XLA Ops:
  0.6 0.0 copy-start.1
  0.6 0.0 copy-start
  2.0 0.1 maximum_convert_fusion
  2.1 0.1 select_reduce_fusion
  2.2 0.7 %convert_bitcast_fusion = f32[8]{0:T(128)S(1)} fusion(s32[1,8]{1,0:T(1,128)} %param.10), kind=kLoop, calls=%fused_computation.7 | loop fusion | flops 8 | bytes 64 | tf_op jit(solution)/shard_map/convert_element_type | solution.py:211
  2.9 0.7 %reshape.100.prior_ref = f32[1,1536]{1,0:T(1,128)S(1)} reshape(f32[1536]{0:T(1024)} %param.15) | data formatting | bytes 12288 | tf_op jit(solution)/shard_map/reshape | solution.py:244
  3.6 0.7 %reduce = f32[1536]{0:T(1024)S(1)} reduce(f32[1,1536]{1,0:T(1,128)} %param.14, f32[]{:T(128)} %constant.29), dimensions={0}, to_apply=%param.14.reduce_sub_computation | reduce | bytes 12292 | tf_op args[6]
  4.3 0.1 broadcast_multiply_fusion.level_ref
  4.4 1.2 %copy.15 = bf16[1,8,16,2,1536]{4,2,3,1,0:T(8,128)(2,1)S(1)} copy(bf16[1,8,16,2,1536]{4,3,2,1,0:T(2,128)(2,1)} %param.8) | data formatting | bytes 1572864 | tf_op args[0]
  5.7 0.0 copy-done.1
  5.7 0.0 copy-done
  5.7 52.4 %shard_map.98 = bf16[8,3,16,1536]{3,2,1,0:T(8,128)(2,1)S(1)} custom-call(f32[1,16]{1,0:T(1,128)S(1)} %bitcast.20, bf16[8,2,16,1536]{3,2,1,0:T(8,128)(2,1)S(1)} %bitcast.17, s32[8,16,1536]{2,1,0:T(8,128)S(1)} %bitcast.18, f32[8,1,1536]{2,1,0:T(1,128)S(1)} %broadcast_multiply_fusion.level_ref, f32[2,1536]{1,0:T(2,128)S(1)} %bitcast.19, ...), custom_call_target="tpu_custom_call" | custom-call | tf_op jit(solution)/shard_map/pallas_call | solution.py:224
  58.1 1.0 %bitcast_convert_fusion = f32[8,16,1536]{2,1,0:T(8,128)} fusion(bf16[8,3,16,1536]{3,2,1,0:T(8,128)(2,1)S(1)} %shard_map.98), kind=kLoop, calls=%fused_computation.2 | loop fusion | flops 196608 | bytes 1179648 | tf_op jit(solution)/shard_map/convert_element_type | solution.py:246
  59.0 0.1 slice_bitcast_fusion
  59.1 1.7 %copy.13 = bf16[8,16,2,1536]{3,2,1,0:T(2,128)(2,1)} copy(bf16[8,16,2,1536]{3,1,2,0:T(8,128)(2,1)S(1)} %slice_bitcast_fusion) | data formatting | bytes 1572864
  (1 shorter events, 0.0 us)
Async XLA Ops:
  0.6 5.0 %copy-start.1 = (f32[1,2,1536]{2,1,0:T(2,128)S(1)}, f32[1,2,1536]{2,1,0:T(2,128)}, u32[]{:S(2)}) copy-start(f32[1,2,1536]{2,1,0:T(2,128)} %param.13) | copy-start | bytes 36868
  0.6 5.0 %copy-start = (s32[1,8,16,1536]{3,2,1,0:T(8,128)S(1)}, s32[1,8,16,1536]{3,2,1,0:T(8,128)}, u32[]{:S(2)}) copy-start(s32[1,8,16,1536]{3,2,1,0:T(8,128)} %param.9) | copy-start | bytes 2359300

commit v3 on v2

--- a/solution.py
+++ b/solution.py
@@ -180,16 +180,17 @@
                 pass_on(t + 1)
         if s > 0:
             pair_sum(s - 1)
-        if p > 0 and k == min(1, chips - 1):
+        if p > 0 and k == 0:
             finish(p - 1)
-        if p > 0 and k == chips - 1:
-            share(p - 1)
+        if p > 1 and k == chips - 1:
+            share(p - 2)
         if s % splits == 0:
             far(t).wait_recv()
         first_part(s)
     pair_sum(steps - 1)
     finish(phases - 1)
-    share(phases - 1)
+    for p in range(max(phases - 2, 0), phases):
+        share(p)
     for p in range(phases):
         for d in range(chips):
             forward(p, d).wait()

time: 61.1 us -> 59.8 us (0.979)
  Pallas kernels: 52.4 us -> 51.1 us
    pallas_call x1, Pallas kernels: 52.4 us -> 51.1 us  [shards(): pl.pallas_call(functools.partial(kernel, lsts, chips, rows, blocks), out_...]
where the time goes in v3:
time: 59.8 us; the launch traced here: 59.5 us
  Pallas kernels  51.1 us (85%)
  local copies, waits for them, and re-layouts  3.7 us (6%)
  other arithmetic  2.59 us (4%)
  between operations  2.1 us (4%)
    pallas_call x1, Pallas kernels, shards(): pl.pallas_call(functools.partial(kernel, lsts, chips, rows, blocks), out_...  51.1 us
    unnamed x6, local copies, waits for them, and re-layouts  2.94 us

profile of v3, /device:TPU:0, one launch (start us, length us, event | category | flops | bytes accessed | tf_op | source)
XLA Modules:
  0.0 59.5 jit_solution(17313247008918571127)
XLA Ops:
  0.6 0.0 copy-start.1
  0.6 0.0 copy-start
  2.0 0.1 maximum_convert_fusion
  2.1 0.1 select_reduce_fusion
  2.2 0.7 %convert_bitcast_fusion = f32[8]{0:T(128)S(1)} fusion(s32[1,8]{1,0:T(1,128)} %param.10), kind=kLoop, calls=%fused_computation.7 | loop fusion | flops 8 | bytes 64 | tf_op jit(solution)/shard_map/convert_element_type | solution.py:212
  2.9 0.7 %reshape.100.prior_ref = f32[1,1536]{1,0:T(1,128)S(1)} reshape(f32[1536]{0:T(1024)} %param.15) | data formatting | bytes 12288 | tf_op jit(solution)/shard_map/reshape | solution.py:245
  3.6 0.7 %reduce = f32[1536]{0:T(1024)S(1)} reduce(f32[1,1536]{1,0:T(1,128)} %param.14, f32[]{:T(128)} %constant.29), dimensions={0}, to_apply=%param.14.reduce_sub_computation | reduce | bytes 12292 | tf_op args[6]
  4.3 0.1 broadcast_multiply_fusion.level_ref
  4.4 1.2 %copy.15 = bf16[1,8,16,2,1536]{4,2,3,1,0:T(8,128)(2,1)S(1)} copy(bf16[1,8,16,2,1536]{4,3,2,1,0:T(2,128)(2,1)} %param.8) | data formatting | bytes 1572864 | tf_op args[0]
  5.7 0.0 copy-done.1
  5.7 0.0 copy-done
  5.7 51.1 %shard_map.98 = bf16[8,3,16,1536]{3,2,1,0:T(8,128)(2,1)S(1)} custom-call(f32[1,16]{1,0:T(1,128)S(1)} %bitcast.20, bf16[8,2,16,1536]{3,2,1,0:T(8,128)(2,1)S(1)} %bitcast.17, s32[8,16,1536]{2,1,0:T(8,128)S(1)} %bitcast.18, f32[8,1,1536]{2,1,0:T(1,128)S(1)} %broadcast_multiply_fusion.level_ref, f32[2,1536]{1,0:T(2,128)S(1)} %bitcast.19, ...), custom_call_target="tpu_custom_call" | custom-call | tf_op jit(solution)/shard_map/pallas_call | solution.py:225
  56.8 1.0 %bitcast_convert_fusion = f32[8,16,1536]{2,1,0:T(8,128)} fusion(bf16[8,3,16,1536]{3,2,1,0:T(8,128)(2,1)S(1)} %shard_map.98), kind=kLoop, calls=%fused_computation.2 | loop fusion | flops 196608 | bytes 1179648 | tf_op jit(solution)/shard_map/convert_element_type | solution.py:247
  57.7 0.1 slice_bitcast_fusion
  57.8 1.7 %copy.13 = bf16[8,16,2,1536]{3,2,1,0:T(2,128)(2,1)} copy(bf16[8,16,2,1536]{3,1,2,0:T(8,128)(2,1)S(1)} %slice_bitcast_fusion) | data formatting | bytes 1572864
  (1 shorter events, 0.0 us)
Async XLA Ops:
  0.6 5.0 %copy-start.1 = (f32[1,2,1536]{2,1,0:T(2,128)S(1)}, f32[1,2,1536]{2,1,0:T(2,128)}, u32[]{:S(2)}) copy-start(f32[1,2,1536]{2,1,0:T(2,128)} %param.13) | copy-start | bytes 36868
  0.6 5.0 %copy-start = (s32[1,8,16,1536]{3,2,1,0:T(8,128)S(1)}, s32[1,8,16,1536]{3,2,1,0:T(8,128)}, u32[]{:S(2)}) copy-start(s32[1,8,16,1536]{3,2,1,0:T(8,128)} %param.9) | copy-start | bytes 2359300
